TPU v7x, 32 devices: a whole 2x2x4 slice. The times are simulated.
32 devices in a mesh: group: 2 (over x), pos: 16 (over z, y, core).
Axes of the slice: x: 2, y: 2, z: 4, core: 2. Of those that a mesh axis runs over, the one named last changes fastest.
Arguments:
- acts: bfloat16 [4, 1024, 1536], P('group', 'pos'), parts along dimension 0, may hold values from -12 to 12
- skips: bfloat16 [4, 2048, 1280], P('group', 'pos'), parts along dimension 0, may hold values from -6 to 6
- norm_gain: float32 [1536], replicated, may hold values from 0.6 to 1.6
- w_query: bfloat16 [1536, 256], replicated, may hold values from -4 to 4
- w_key: bfloat16 [1536, 256], replicated, may hold values from -4 to 4
- w_value: bfloat16 [1536, 768], replicated, may hold values from -0.15625 to 0.15625
- w_out: bfloat16 [768, 1536], replicated, may hold values from -0.21875 to 0.21875
- w_lift: bfloat16 [1536, 1536], P('pos'), may hold values from -0.15625 to 0.15625
- w_skip: bfloat16 [1280, 1536], P('pos'), may hold values from -0.15625 to 0.15625
- depth_kernel: float32 [3, 1536], replicated, may hold values from -3 to 3
- w_point: bfloat16 [1536, 1536], P(None, 'pos'), may hold values from -0.15625 to 0.15625
Outputs:
- decoded: bfloat16 [4, 2048, 1536], P('group', 'pos'), parts along dimension 0
There are 2 independent parts, one for each index of `group`. A program takes and returns all parts, laid end to end along the dimension named above; an argument that names none is the same for every part. Nothing has to cross between parts.
All inputs are finite; a program needn't handle non-finite values.
Results may differ from a plain program's by a relative error of at most 0.014.
Values may be sent and summed in bfloat16 or wider, within the bound.
A program may use at most 128 MiB of HBM per device.

v0:
```python
import jax
import jax.numpy as jnp
from jax import lax
from jax.sharding import PartitionSpec as P

HEADS = 4
HK = 64
HV = 192


def extended(cells, sides, width):
    for axis, dim in sides:
        count = lax.axis_size(axis)
        ends = count - 1
        head = lax.slice_in_dim(cells, 0, width, axis=dim)
        tail = lax.slice_in_dim(cells, cells.shape[dim] - width, cells.shape[dim], axis=dim)
        cells = jnp.concatenate(
            [
                lax.ppermute(tail, axis, [(i, (i + 1) % count) for i in range(ends)]),
                cells,
                lax.ppermute(head, axis, [((i + 1) % count, i) for i in range(ends)]),
            ],
            axis=dim,
        )
    return cells


def on_device(
    acts, skips, norm_gain, w_query, w_key, w_value, w_out, w_lift, w_skip, depth_kernel, w_point
):
    lift_full, skip_full, point_full = (
        lax.all_gather(w_lift, "pos", axis=0, tiled=True),
        lax.all_gather(w_skip, "pos", axis=0, tiled=True),
        lax.all_gather(w_point, "pos", axis=1, tiled=True),
    )
    seq_count, bin_rows, width = acts.shape
    actsf = acts.astype(jnp.float32)
    centre = actsf - jnp.mean(actsf, axis=-1, keepdims=True)
    normed = (
        centre * lax.rsqrt(jnp.mean(centre * centre, axis=-1, keepdims=True) + 1e-05) * norm_gain
    ).astype(jnp.bfloat16)
    flat = normed.reshape(seq_count * bin_rows, width)
    queries = (
        (jnp.dot(flat, w_query, preferred_element_type=jnp.float32) * HK ** (-0.5))
        .astype(jnp.bfloat16)
        .reshape(seq_count, bin_rows, HEADS, HK)
    )
    keys_here = (
        jnp.dot(flat, w_key, preferred_element_type=jnp.float32)
        .astype(jnp.bfloat16)
        .reshape(seq_count, bin_rows, HEADS * HK)
    )
    values_here = (
        jnp.dot(flat, w_value, preferred_element_type=jnp.float32)
        .astype(jnp.bfloat16)
        .reshape(seq_count, bin_rows, HEADS * HV)
    )
    running = jnp.full((seq_count, HEADS, bin_rows), -1e30, jnp.float32)
    key_piece = lax.all_gather(keys_here, "pos", axis=1, tiled=True)
    value_piece = lax.all_gather(values_here, "pos", axis=1, tiled=True)
    count = key_piece.shape[1]
    keyed = key_piece.reshape(seq_count, count, HEADS, HK)
    valued = value_piece.reshape(seq_count, count, HEADS, HV)
    scores = jnp.einsum("sqhd,skhd->shqk", queries, keyed, preferred_element_type=jnp.float32)
    newest = jnp.maximum(running, jnp.max(scores, axis=-1))
    weights = jnp.exp(scores - newest[..., None])
    totals = jnp.sum(weights, axis=-1)
    summed = jnp.einsum(
        "shqk,skhv->shqv", weights.astype(jnp.bfloat16), valued, preferred_element_type=jnp.float32
    )
    running, totals, summed = (newest, totals, summed)
    mixed = (
        (summed / totals[..., None])
        .transpose(0, 2, 1, 3)
        .reshape(seq_count * bin_rows, HEADS * HV)
        .astype(jnp.bfloat16)
    )
    attended = (
        actsf.reshape(seq_count * bin_rows, width)
        + jnp.dot(mixed, w_out, preferred_element_type=jnp.float32)
    ).astype(jnp.bfloat16)
    activated = jax.nn.gelu(attended.astype(jnp.float32)).astype(jnp.bfloat16)
    lifted = jnp.dot(activated, lift_full, preferred_element_type=jnp.float32)
    lifted = lifted.astype(jnp.bfloat16).reshape(seq_count, bin_rows, width)
    raised = jnp.repeat(lifted, 2, axis=1).reshape(seq_count * 2 * bin_rows, width)
    skip_act = (
        jax.nn.gelu(skips.astype(jnp.float32))
        .astype(jnp.bfloat16)
        .reshape(seq_count * 2 * bin_rows, skips.shape[2])
    )
    skip_term = jnp.dot(skip_act, skip_full, preferred_element_type=jnp.float32)
    merged = (
        (raised.astype(jnp.float32) + skip_term)
        .astype(jnp.bfloat16)
        .reshape(seq_count, 2 * bin_rows, width)
    )
    padded = extended(merged, (("pos", 1),), 1)
    paddedf = padded.astype(jnp.float32)
    spread = (
        depth_kernel[0] * paddedf[:, :-2]
        + depth_kernel[1] * paddedf[:, 1:-1]
        + depth_kernel[2] * paddedf[:, 2:]
    ).astype(jnp.bfloat16)
    spread = spread.reshape(seq_count * 2 * bin_rows, width)
    decoded = jnp.dot(spread, point_full, preferred_element_type=jnp.float32)
    return decoded.astype(jnp.bfloat16).reshape(seq_count, 2 * bin_rows, width)


def solution(mesh):
    return jax.shard_map(
        on_device,
        mesh=mesh,
        in_specs=(
            P("group", "pos", None),
            P("group", "pos", None),
            P(),
            P(),
            P(),
            P(),
            P(),
            P("pos", None),
            P("pos", None),
            P(),
            P(None, "pos"),
        ),
        out_specs=P("group", "pos", None),
        check_vma=False,
    )
```

profile of v0, /device:TPU:0, one launch (start us, length us, event | category | flops | bytes accessed | tf_op | source)
XLA Modules:
  0.0 268.4 jit_solution(8063212985456525454)
XLA Ops:
  6.5 0.0 copy-start
  6.5 0.0 copy-start.3
  6.5 0.0 all-gather.6.cloned.1.call-start
  6.5 1.3 convert_reduce_fusion
  7.8 1.3 multiply_reduce_fusion
  9.1 1.3 multiply_convert_fusion
  10.4 0.0 copy-done.3
  10.4 0.9 convolution_convert_fusion.3
  11.3 0.0 all-gather.6.cloned.1.call-update
  11.3 0.0 copy-start.4
  11.3 0.0 all-gather.8.cloned.1.call-start
  11.4 2.9 %convolution_convert_fusion.2 = bf16[128,768]{1,0:T(8,128)(2,1)} fusion(bf16[128,1536]{1,0:T(8,128)(2,1)S(1)} %bitcast.36, bf16[1536,768]{1,0:T(8,128)(2,1)} %param.16), kind=kOutput, calls=%fused_computation.30 | convolution fusion | flops 302088192 | bytes 2949120 | tf_op jit(solution)/shard_map/dot_general | solution.py:54
  14.3 0.0 all-gather.8.cloned.1.call-update
  14.3 0.0 all-gather.10.cloned.1.call-start
  14.3 0.7 all-gather.10.cloned.1.call-update
  15.0 0.0 all-gather.12.cloned.1.call-start
  15.1 0.5 all-gather.12.cloned.1.call-update
  15.6 0.0 all-gather.14.cloned.1.call-start
  15.6 0.5 all-gather.14.cloned.1.call-update
  16.2 0.0 copy-done.4
  16.2 0.9 fusion.16
  17.1 1.0 reshape.61
  18.1 2.4 fusion.13
  20.4 31.7 %all-gather.6.cloned.1.call-done = bf16[2,1024,256]{2,1,0:T(8,128)(2,1)} async-done(((bf16[2,64,256]{2,1,0:T(8,128)(2,1)}), bf16[2,1024,256]{2,1,0:T(8,128)(2,1)}) %all-gather.6.cloned.1.call-update) | async-done | bytes 1048592 | tf_op jit(solution)/shard_map/all_gather | solution.py:59
  52.1 1.5 copy.15
  53.6 0.5 fusion.38
  54.1 0.0 copy-start.1
  54.1 1.3 copy-done.1
  55.5 0.5 fusion.3
  56.0 42.6 %all-gather.8.cloned.1.call-done = bf16[2,1024,768]{2,1,0:T(8,128)(2,1)} async-done(((bf16[2,64,768]{2,1,0:T(8,128)(2,1)}), bf16[2,1024,768]{2,1,0:T(8,128)(2,1)}) %all-gather.8.cloned.1.call-update) | async-done | bytes 3145744 | tf_op jit(solution)/shard_map/all_gather | solution.py:60
  98.6 4.6 %copy.17 = bf16[2,1024,768]{1,2,0:T(8,128)(2,1)} copy(bf16[2,1024,768]{2,1,0:T(8,128)(2,1)} %all-gather.8.cloned.1.call-done) | data formatting | bytes 6291456 | tf_op jit(solution)/shard_map/all_gather | solution.py:60
  103.2 0.0 copy-start.2
  103.2 3.7 %fusion.15 = bf16[2,64,4,192]{3,1,2,0:T(8,128)(2,1)S(1)} fusion(bf16[2,1024,4,192]{1,3,2,0:T(8,128)(2,1)} %bitcast.40, f32[2,4,64,1024]{3,2,1,0:T(8,128)} %copy-done.1, f32[2,4,64]{2,1,0:T(4,128)S(1)} %broadcast_maximum_fusion, f32[2,64,4]{1,2,0:T(4,128)S(1)} %bitcast.48), kind=kOutput, calls=%fused_computation.28 | convolution fusion | flops 202571776 | bytes 5443584 | tf_op jit(solution)/shard_map/shqk,skhv->shqv/dot_general | solution.py:68
  106.9 0.2 copy.18
  107.2 0.2 convert_element_type.71
  107.4 45.7 %all-gather.10.cloned.1.call-done = bf16[1536,1536]{1,0:T(8,128)(2,1)} async-done(((bf16[96,1536]{1,0:T(8,128)(2,1)}), bf16[1536,1536]{1,0:T(8,128)(2,1)}) %all-gather.10.cloned.1.call-update) | async-done | bytes 4718608 | tf_op jit(solution)/shard_map/all_gather | solution.py:32
  153.1 0.0 copy-done
  153.1 0.0 copy-done.2
  153.1 3.7 %convolution_convert_fusion.1 = bf16[128,1536]{1,0:T(8,128)(2,1)S(1)} fusion(bf16[1536,1536]{1,0:T(8,128)(2,1)} %all-gather.10.cloned.1.call-done, bf16[128,768]{1,0:T(8,128)(2,1)S(1)} %convert_element_type.71, bf16[768,1536]{1,0:T(8,128)(2,1)S(1)} %copy-done, bf16[128,1536]{1,0:T(8,128)(2,1)S(1)} %bitcast.39), kind=kOutput, calls=%fused_computation.6 | convolution fusion | flops 908722176 | bytes 8060928 | tf_op jit(solution)/shard_map/dot_general | solution.py:83
  156.8 1.6 broadcast_in_dim.5
  158.3 0.0 copy-start.5
  158.3 3.2 %convert_element_type.78 = f32[256,1536]{1,0:T(8,128)} reshape(f32[2,64,2,1536]{3,2,1,0:T(2,128)} %broadcast_in_dim.5) | data formatting | bytes 3145728 | tf_op jit(solution)/shard_map/convert_element_type | solution.py:93
  161.5 41.0 %all-gather.12.cloned.1.call-done = bf16[1280,1536]{1,0:T(8,128)(2,1)} async-done(((bf16[80,1536]{1,0:T(8,128)(2,1)}), bf16[1280,1536]{1,0:T(8,128)(2,1)}) %all-gather.12.cloned.1.call-update) | async-done | bytes 3932176 | tf_op jit(solution)/shard_map/all_gather | solution.py:33
  202.6 0.0 copy-done.5
  202.6 0.0 copy-start.6
  202.6 3.8 %fusion = bf16[256,1536]{1,0:T(8,128)(2,1)S(1)} fusion(f32[256,1536]{1,0:T(8,128)} %convert_element_type.78, bf16[256,1280]{1,0:T(8,128)(2,1)S(1)} %bitcast.45, bf16[1280,1536]{1,0:T(8,128)(2,1)} %all-gather.12.cloned.1.call-done), kind=kOutput, calls=%fused_computation.1 | convolution fusion | flops 1007419392 | bytes 6946816 | tf_op jit(solution)/shard_map/dot_general | solution.py:91
  206.4 2.2 collective-permute-start
  208.6 1.3 collective-permute-start.1
  209.9 0.0 copy-done.6
  209.9 0.1 slice_reduce_fusion.2
  209.9 0.0 collective-permute-done
  210.0 1.7 collective-permute-done.1
  211.7 0.2 maximum_convert_fusion
  211.9 0.5 fusion.6
  212.4 44.8 %all-gather.14.cloned.1.call-done = bf16[1536,1536]{0,1:T(8,128)(2,1)} async-done(((bf16[1536,96]{0,1:T(8,128)(2,1)}), bf16[1536,1536]{0,1:T(8,128)(2,1)}) %all-gather.14.cloned.1.call-update) | async-done | bytes 4718608 | tf_op jit(solution)/shard_map/all_gather | solution.py:34
  257.2 4.6 %convolution_convert_fusion = bf16[256,1536]{1,0:T(8,128)(2,1)} fusion(bf16[256,1536]{1,0:T(8,128)(2,1)S(1)} %bitcast.44, bf16[1536,1536]{0,1:T(8,128)(2,1)} %all-gather.14.cloned.1.call-done), kind=kOutput, calls=%fused_computation.2 | convolution fusion | flops 1208352768 | bytes 6291456 | tf_op jit(solution)/shard_map/dot_general | solution.py:105
  (4 shorter events, 0.0 us)
Async XLA Ops:
  6.5 146.6 %copy-start = (bf16[768,1536]{1,0:T(8,128)(2,1)S(1)}, bf16[768,1536]{1,0:T(8,128)(2,1)}, u32[]{:S(2)}) copy-start(bf16[768,1536]{1,0:T(8,128)(2,1)} %param.17) | copy-start | bytes 7077892
  6.5 3.8 %copy-start.3 = (bf16[1536,256]{1,0:T(8,128)(2,1)S(1)}, bf16[1536,256]{1,0:T(8,128)(2,1)}, u32[]{:S(2)}) copy-start(bf16[1536,256]{1,0:T(8,128)(2,1)} %param.15) | copy-start | bytes 2359300
  6.5 45.6 %all-gather.6.cloned.1.call-start = ((), (), s32[]{:S(2)}) async-start(), calls=%async_computation | async-start | bytes 1114112 | tf_op jit(solution)/shard_map/all_gather | solution.py:59
  11.3 4.9 %copy-start.4 = (bf16[1536,256]{1,0:T(8,128)(2,1)S(1)}, bf16[1536,256]{1,0:T(8,128)(2,1)}, u32[]{:S(2)}) copy-start(bf16[1536,256]{1,0:T(8,128)(2,1)} %param.14) | copy-start | bytes 2359300
  11.3 87.3 %all-gather.8.cloned.1.call-start = ((), (), s32[]{:S(2)}) async-start(), calls=%async_computation.1 | async-start | bytes 3342336 | tf_op jit(solution)/shard_map/all_gather | solution.py:60
  14.3 138.8 %all-gather.10.cloned.1.call-start = ((), (), s32[]{:S(2)}) async-start(), calls=%async_computation.2 | async-start | bytes 5013504 | tf_op jit(solution)/shard_map/all_gather | solution.py:32
  15.0 187.6 %all-gather.12.cloned.1.call-start = ((), (), s32[]{:S(2)}) async-start(), calls=%async_computation.3 | async-start | bytes 4177920 | tf_op jit(solution)/shard_map/all_gather | solution.py:33
  15.6 241.7 %all-gather.14.cloned.1.call-start = ((), (), s32[]{:S(2)}) async-start(), calls=%async_computation.4 | async-start | bytes 5013504 | tf_op jit(solution)/shard_map/all_gather | solution.py:34
  54.1 1.4 copy-start.1
  103.2 49.9 %copy-start.2 = (bf16[2,64,1536]{2,1,0:T(8,128)(2,1)S(1)}, bf16[2,64,1536]{2,1,0:T(8,128)(2,1)}, u32[]{:S(2)}) copy-start(bf16[2,64,1536]{2,1,0:T(8,128)(2,1)} %param.11) | copy-start | bytes 1179652
  158.3 44.3 %copy-start.5 = (bf16[2,128,1280]{2,1,0:T(8,128)(2,1)S(1)}, bf16[2,128,1280]{2,1,0:T(8,128)(2,1)}, u32[]{:S(2)}) copy-start(bf16[2,128,1280]{2,1,0:T(8,128)(2,1)} %fusion.13) | copy-start | bytes 1966084
  202.6 7.3 %copy-start.6 = (f32[3,1536]{1,0:T(4,128)S(1)}, f32[3,1536]{1,0:T(4,128)}, u32[]{:S(2)}) copy-start(f32[3,1536]{1,0:T(4,128)} %param.20) | copy-start | bytes 55300
  206.4 3.5 %collective-permute-start = (bf16[2,1,1536]{2,1,0:T(2,128)(2,1)S(1)}, bf16[2,1,1536]{2,1,0:T(2,128)(2,1)S(1)}, u32[]{:S(2)}, u32[]{:S(2)}) collective-permute-start(bf16[2,1,1536]{2,1,0:T(2,128)(2,1)S(1)} %get-tuple-element.8), channel_id=1, source_target_pairs={{0,1},{1,2},{2,3},{3,4},{4,5},{5,6},{6,7},{7,8},{8,9},{9,10},{10,1... | collective-permute-start | bytes 18440 | tf_op jit(solution)/shard_map/ppermute | solution.py:19
  208.6 3.1 %collective-permute-start.1 = (bf16[2,1,1536]{2,1,0:T(2,128)(2,1)S(1)}, bf16[2,1,1536]{2,1,0:T(2,128)(2,1)S(1)}, u32[]{:S(2)}, u32[]{:S(2)}) collective-permute-start(bf16[2,1,1536]{2,1,0:T(2,128)(2,1)S(1)} %get-tuple-element.9), channel_id=1, source_target_pairs={{1,0},{2,1},{3,2},{4,3},{5,4},{6,5},{7,6},{8,7},{9,8},{10,9},{11,1... | collective-permute-start | bytes 18440 | tf_op jit(solution)/shard_map/ppermute | solution.py:21
Sparse Core Ops, SparseCore 0:
  11.4 40.6 all-gather.5
  54.4 44.1 all-gather.7
  100.9 52.1 all-gather.9
  155.2 47.3 all-gather.11
  204.7 52.4 all-gather.13
where the time goes:
time: 269 us; the launch traced here: 268 us
  waiting for transfers between devices  209 us (78%)
  matrix products  21 us (8%)
  local copies, waits for them, and re-layouts  13.7 us (5%)
  between operations  13.3 us (5%)
  other arithmetic  7.44 us (3%)
  starting transfers between devices  3.61 us (1%)
    all_gather x1, waiting for transfers between devices, on_device(): lax.all_gather(w_lift, 'pos', axis=0, tiled=True)  45.7 us
    all_gather x1, waiting for transfers between devices, on_device(): lax.all_gather(w_point, 'pos', axis=1, tiled=True)  44.8 us
    all_gather x1, waiting for transfers between devices, on_device(): value_piece = lax.all_gather(values_here, 'pos', axis=1, tiled=True)  42.6 us
    all_gather x1, waiting for transfers between devices, on_device(): lax.all_gather(w_skip, 'pos', axis=0, tiled=True)  41 us
    all_gather x1, waiting for transfers between devices, on_device(): key_piece = lax.all_gather(keys_here, 'pos', axis=1, tiled=True)  31.7 us
  transfers between devices with their start and end apart: 7, of which 6 were waited for; matrix products, arithmetic and copies ran while one was open for 12% of the time, Pallas kernels for 0%

commit v1 on v0

--- a/solution.py
+++ b/solution.py
@@ -6,6 +6,27 @@
 HEADS = 4
 HK = 64
 HV = 192
+
+
+def gather_around(array, axis, dim):
+    length, index, rows = (lax.axis_size(axis), lax.axis_index(axis), array.shape[dim])
+    ahead = [(i, (i + 1) % length) for i in range(length)]
+    left = [(i, (i - 1) % length) for i in range(length)]
+    result = jnp.zeros((*array.shape[:dim], length * rows, *array.shape[dim + 1 :]), array.dtype)
+    result = lax.dynamic_update_slice_in_dim(result, array, index * rows, axis=dim)
+    from_left = from_right = array
+    middle = length // 2
+    for turn in range(1, middle + 1):
+        from_left = lax.ppermute(from_left, axis, ahead)
+        result = lax.dynamic_update_slice_in_dim(
+            result, from_left, (index - turn) % length * rows, axis=dim
+        )
+        if turn < length - middle:
+            from_right = lax.ppermute(from_right, axis, left)
+            result = lax.dynamic_update_slice_in_dim(
+                result, from_right, (index + turn) % length * rows, axis=dim
+            )
+    return result
 
 
 def extended(cells, sides, width):
@@ -56,7 +77,7 @@
         .reshape(seq_count, bin_rows, HEADS * HV)
     )
     running = jnp.full((seq_count, HEADS, bin_rows), -1e30, jnp.float32)
-    key_piece = lax.all_gather(keys_here, "pos", axis=1, tiled=True)
+    key_piece = gather_around(keys_here, "pos", 1)
     value_piece = lax.all_gather(values_here, "pos", axis=1, tiled=True)
     count = key_piece.shape[1]
     keyed = key_piece.reshape(seq_count, count, HEADS, HK)

time: 269 us -> 236 us (0.88)
  waiting for transfers between devices: 209 us -> 96.6 us
  local copies, waits for them, and re-layouts: 13.7 us -> 60.5 us
  starting transfers between devices: 3.61 us -> 37.1 us
    all_gather x1, waiting for transfers between devices: 45.7 us -> 0.02 us  [on_device(): lax.all_gather(w_lift, 'pos', axis=0, tiled=True)]
    all_gather x1, waiting for transfers between devices: 42.6 us -> 0.02 us  [on_device(): value_piece = lax.all_gather(values_here, 'pos', axis=1, tiled=True)]
    ppermute x0 -> x15, starting transfers between devices: none -> 33.5 us  [the longest x7 33 us: gather_around(): from_right = lax.ppermute(from_right, axis, left)]
    all_gather x1 -> x0, waiting for transfers between devices: 31.7 us -> none  [on_device(): key_piece = lax.all_gather(keys_here, 'pos', axis=1, tiled=True)]
    dynamic_update_slice x0 -> x16, local copies, waits for them, and re-layouts: none -> 24.1 us  [the longest x8 11.9 us: gather_around(): lax.dynamic_update_slice_in_dim(result, from_left, (index - turn) % lengt...]
    ppermute x0 -> x15, local copies, waits for them, and re-layouts: none -> 23.8 us  [the longest x8 12.7 us: gather_around(): from_left = lax.ppermute(from_left, axis, ahead)]
    ppermute x0 -> x15, waiting for transfers between devices: none -> 12.9 us  [the longest x8 7.46 us: gather_around(): from_left = lax.ppermute(from_left, axis, ahead)]
    all_gather x1, waiting for transfers between devices: 41 us -> 35.2 us  [on_device(): lax.all_gather(w_skip, 'pos', axis=0, tiled=True)]
  transfers between devices with their start and end apart: 7 -> 21, of which waited for: 6 -> 15; matrix products, arithmetic and copies ran while one was open for 12% -> 32% of each run, Pallas kernels for 0% -> 0%
where the time goes in v1:
time: 236 us; the launch traced here: 235 us
  waiting for transfers between devices  96.6 us (41%)
  local copies, waits for them, and re-layouts  60.5 us (26%)
  starting transfers between devices  37.1 us (16%)
  matrix products  19.8 us (8%)
  between operations  13.7 us (6%)
  other arithmetic  7.46 us (3%)
    all_gather x1, waiting for transfers between devices, on_device(): lax.all_gather(w_point, 'pos', axis=1, tiled=True)  44.9 us
    all_gather x1, waiting for transfers between devices, on_device(): lax.all_gather(w_skip, 'pos', axis=0, tiled=True)  35.2 us
    ppermute x7, starting transfers between devices, gather_around(): from_right = lax.ppermute(from_right, axis, left)  33 us
    ppermute x8, local copies, waits for them, and re-layouts, gather_around(): from_left = lax.ppermute(from_left, axis, ahead)  12.7 us
    dynamic_update_slice x8, local copies, waits for them, and re-layouts, gather_around(): lax.dynamic_update_slice_in_dim(result, from_left, (index - turn) % lengt...  11.9 us
    ppermute x7, local copies, waits for them, and re-layouts, gather_around(): from_right = lax.ppermute(from_right, axis, left)  11.1 us
    dynamic_update_slice x7, local copies, waits for them, and re-layouts, gather_around(): lax.dynamic_update_slice_in_dim(result, from_right, (index + turn) % leng...  10.8 us
    ppermute x8, waiting for transfers between devices, gather_around(): from_left = lax.ppermute(from_left, axis, ahead)  7.46 us
  transfers between devices with their start and end apart: 21, of which 15 were waited for; matrix products, arithmetic and copies ran while one was open for 32% of the time, Pallas kernels for 0%

profile of v1, /device:TPU:0, one launch (start us, length us, event | category | flops | bytes accessed | tf_op | source)
XLA Modules:
  0.0 235.1 jit_solution(16190436364745730499)
XLA Ops:
  6.5 1.3 convert_reduce_fusion
  7.8 1.3 multiply_reduce_fusion
  9.1 1.3 multiply_convert_fusion
  10.4 2.9 %convolution_convert_fusion.2 = bf16[128,768]{1,0:T(8,128)(2,1)} fusion(bf16[128,1536]{1,0:T(8,128)(2,1)S(1)} %bitcast.35, bf16[1536,768]{1,0:T(8,128)(2,1)} %param.16), kind=kOutput, calls=%fused_computation.30 | convolution fusion | flops 302088192 | bytes 2949120 | tf_op jit(solution)/shard_map/dot_general | solution.py:75
  16.3 5.4 %collective-permute-start.1 = (bf16[2,64,256]{2,1,0:T(8,128)(2,1)S(1)}, bf16[2,64,256]{2,1,0:T(8,128)(2,1)S(1)}, u32[]{:S(2)}, u32[]{:S(2)}) collective-permute-start(bf16[2,64,256]{2,1,0:T(8,128)(2,1)S(1)} %bitcast.48), channel_id=1, source_target_pairs={{0,15},{1,0},{2,1},{3,2},{4,3},{5,4},{6,5},{7,6},{8,7},{9,8},{10,9... | collective-permute-start | bytes 196616 | tf_op jit(solution)/shard_map/ppermute | solution.py:25
  21.7 1.5 collective-permute-done
  23.6 4.5 %collective-permute-start.3 = (bf16[2,64,256]{2,1,0:T(8,128)(2,1)S(1)}, bf16[2,64,256]{2,1,0:T(8,128)(2,1)S(1)}, u32[]{:S(2)}, u32[]{:S(2)}) collective-permute-start(bf16[2,64,256]{2,1,0:T(8,128)(2,1)S(1)} %collective-permute-done.1), channel_id=1, source_target_pairs={{0,15},{1,0},{2,1},{3,2},{4,3},{5,4},{6,5},{7,6},{8,7},{9,8},{10,9... | collective-permute-start | bytes 196616 | tf_op jit(solution)/shard_map/ppermute | solution.py:25
  28.1 1.7 collective-permute-done.2
  29.9 1.2 collective-permute-done.3
  31.0 4.7 %collective-permute-start.5 = (bf16[2,64,256]{2,1,0:T(8,128)(2,1)S(1)}, bf16[2,64,256]{2,1,0:T(8,128)(2,1)S(1)}, u32[]{:S(2)}, u32[]{:S(2)}) collective-permute-start(bf16[2,64,256]{2,1,0:T(8,128)(2,1)S(1)} %collective-permute-done.3), channel_id=1, source_target_pairs={{0,15},{1,0},{2,1},{3,2},{4,3},{5,4},{6,5},{7,6},{8,7},{9,8},{10,9... | collective-permute-start | bytes 196616 | tf_op jit(solution)/shard_map/ppermute | solution.py:25
  36.7 1.0 collective-permute-done.5
  37.6 4.5 %collective-permute-start.7 = (bf16[2,64,256]{2,1,0:T(8,128)(2,1)S(1)}, bf16[2,64,256]{2,1,0:T(8,128)(2,1)S(1)}, u32[]{:S(2)}, u32[]{:S(2)}) collective-permute-start(bf16[2,64,256]{2,1,0:T(8,128)(2,1)S(1)} %collective-permute-done.5), channel_id=1, source_target_pairs={{0,15},{1,0},{2,1},{3,2},{4,3},{5,4},{6,5},{7,6},{8,7},{9,8},{10,9... | collective-permute-start | bytes 196616 | tf_op jit(solution)/shard_map/ppermute | solution.py:25
  42.1 1.0 collective-permute-done.6
  43.2 1.8 collective-permute-done.7
  45.0 4.7 %collective-permute-start.9 = (bf16[2,64,256]{2,1,0:T(8,128)(2,1)S(1)}, bf16[2,64,256]{2,1,0:T(8,128)(2,1)S(1)}, u32[]{:S(2)}, u32[]{:S(2)}) collective-permute-start(bf16[2,64,256]{2,1,0:T(8,128)(2,1)S(1)} %collective-permute-done.7), channel_id=1, source_target_pairs={{0,15},{1,0},{2,1},{3,2},{4,3},{5,4},{6,5},{7,6},{8,7},{9,8},{10,9... | collective-permute-start | bytes 196616 | tf_op jit(solution)/shard_map/ppermute | solution.py:25
  49.7 1.1 collective-permute-done.8
  50.8 1.1 collective-permute-done.9
  51.9 4.8 %collective-permute-start.11 = (bf16[2,64,256]{2,1,0:T(8,128)(2,1)S(1)}, bf16[2,64,256]{2,1,0:T(8,128)(2,1)}, u32[]{:S(2)}, u32[]{:S(2)}) collective-permute-start(bf16[2,64,256]{2,1,0:T(8,128)(2,1)S(1)} %collective-permute-done.9), channel_id=1, source_target_pairs={{0,15},{1,0},{2,1},{3,2},{4,3},{5,4},{6,5},{7,6},{8,7},{9,8},{10,9... | collective-permute-start | bytes 196616 | tf_op jit(solution)/shard_map/ppermute | solution.py:25
  57.5 2.4 %fusion.13 = bf16[2,128,1280]{2,1,0:T(8,128)(2,1)} fusion(bf16[2,128,1280]{2,1,0:T(8,128)(2,1)} %param.12), kind=kLoop, calls=%fused_computation.25 | loop fusion | flops 3276800 | bytes 1310720 | tf_op jit(solution)/shard_map/convert_element_type | solution.py:109
  59.9 4.4 %collective-permute-start.13 = (bf16[2,64,256]{2,1,0:T(8,128)(2,1)}, bf16[2,64,256]{2,1,0:T(8,128)(2,1)}, u32[]{:S(2)}, u32[]{:S(2)}) collective-permute-start(bf16[2,64,256]{2,1,0:T(8,128)(2,1)} %collective-permute-done.11), channel_id=1, source_target_pairs={{0,15},{1,0},{2,1},{3,2},{4,3},{5,4},{6,5},{7,6},{8,7},{9,8},{10,9... | collective-permute-start | bytes 196616 | tf_op jit(solution)/shard_map/ppermute | solution.py:25
  66.0 1.4 dynamic_update_slice.48
  67.5 1.6 copy.31
  69.1 1.7 dynamic_update_slice.49
  70.8 1.6 copy.32
  72.4 1.8 dynamic_update_slice.50
  74.2 1.6 copy.33
  75.8 1.2 dynamic_update_slice.51
  76.9 1.6 copy.34
  78.5 1.2 dynamic_update_slice.52
  79.8 1.6 copy.35
  81.4 1.8 dynamic_update_slice.53
  83.1 1.6 copy.36
  84.7 1.8 dynamic_update_slice.54
  86.5 1.6 copy.37
  88.1 1.2 dynamic_update_slice.55
  89.3 1.6 copy.38
  90.9 1.2 dynamic_update_slice.56
  92.1 1.6 copy.39
  93.7 1.8 dynamic_update_slice.57
  95.5 1.6 copy.40
  97.1 1.8 dynamic_update_slice.58
  98.9 1.6 copy.41
  100.5 1.2 dynamic_update_slice.59
  101.7 1.6 copy.42
  103.3 1.2 dynamic_update_slice.60
  104.5 1.6 copy.43
  106.1 1.8 dynamic_update_slice.61
  107.9 1.6 copy.44
  109.5 1.8 dynamic_update_slice.62
  111.3 1.6 copy.45
  112.9 1.2 dynamic_update_slice.63
  114.6 1.4 copy-done.1
  116.5 4.7 %copy.47 = bf16[2,1024,768]{1,2,0:T(8,128)(2,1)} copy(bf16[2,1024,768]{2,1,0:T(8,128)(2,1)} %all-gather.5.cloned.1.call-done) | data formatting | bytes 6291456 | tf_op jit(solution)/shard_map/all_gather | solution.py:81
  121.3 3.7 %fusion.15 = bf16[2,64,4,192]{3,1,2,0:T(8,128)(2,1)S(1)} fusion(bf16[2,1024,4,192]{1,3,2,0:T(8,128)(2,1)} %bitcast.40, f32[2,4,64,1024]{3,2,1,0:T(8,128)} %copy-done.1, f32[2,4,64]{2,1,0:T(4,128)S(1)} %broadcast_maximum_fusion, f32[2,64,4]{1,2,0:T(4,128)S(1)} %bitcast.50), kind=kOutput, calls=%fused_computation.28 | convolution fusion | flops 202571776 | bytes 5443584 | tf_op jit(solution)/shard_map/shqk,skhv->shqv/dot_general | solution.py:89
  125.5 3.7 %convolution_convert_fusion.1 = bf16[128,1536]{1,0:T(8,128)(2,1)S(1)} fusion(bf16[1536,1536]{1,0:T(8,128)(2,1)} %all-gather.7.cloned.1.call-done, bf16[128,768]{1,0:T(8,128)(2,1)S(1)} %convert_element_type.71, bf16[768,1536]{1,0:T(8,128)(2,1)S(1)} %copy-done, bf16[128,1536]{1,0:T(8,128)(2,1)S(1)} %bitcast.39), kind=kOutput, calls=%fused_computation.6 | convolution fusion | flops 908722176 | bytes 8060928 | tf_op jit(solution)/shard_map/dot_general | solution.py:104
  129.2 1.6 broadcast_in_dim.16
  130.8 3.3 %convert_element_type.78 = f32[256,1536]{1,0:T(8,128)} reshape(f32[2,64,2,1536]{3,2,1,0:T(2,128)} %broadcast_in_dim.16) | data formatting | bytes 3145728 | tf_op jit(solution)/shard_map/convert_element_type | solution.py:114
  134.0 35.2 %all-gather.9.cloned.1.call-done = bf16[1280,1536]{1,0:T(8,128)(2,1)} async-done(((bf16[80,1536]{1,0:T(8,128)(2,1)}), bf16[1280,1536]{1,0:T(8,128)(2,1)}) %all-gather.9.cloned.1.call-update) | async-done | bytes 3932176 | tf_op jit(solution)/shard_map/all_gather | solution.py:54
  169.3 3.8 %fusion = bf16[256,1536]{1,0:T(8,128)(2,1)S(1)} fusion(f32[256,1536]{1,0:T(8,128)} %convert_element_type.78, bf16[256,1280]{1,0:T(8,128)(2,1)S(1)} %bitcast.45, bf16[1280,1536]{1,0:T(8,128)(2,1)} %all-gather.9.cloned.1.call-done), kind=kOutput, calls=%fused_computation.1 | convolution fusion | flops 1007419392 | bytes 6946816 | tf_op jit(solution)/shard_map/dot_general | solution.py:112
  173.1 2.2 collective-permute-start.15
  175.2 1.3 collective-permute-start.16
  176.6 1.7 collective-permute-done.16
  179.1 44.9 %all-gather.11.cloned.1.call-done = bf16[1536,1536]{0,1:T(8,128)(2,1)} async-done(((bf16[1536,96]{0,1:T(8,128)(2,1)}), bf16[1536,1536]{0,1:T(8,128)(2,1)}) %all-gather.11.cloned.1.call-update) | async-done | bytes 4718608 | tf_op jit(solution)/shard_map/all_gather | solution.py:55
  223.9 4.6 %convolution_convert_fusion = bf16[256,1536]{1,0:T(8,128)(2,1)} fusion(bf16[256,1536]{1,0:T(8,128)(2,1)S(1)} %bitcast.44, bf16[1536,1536]{0,1:T(8,128)(2,1)} %all-gather.11.cloned.1.call-done), kind=kOutput, calls=%fused_computation.2 | convolution fusion | flops 1208352768 | bytes 6291456 | tf_op jit(solution)/shard_map/dot_general | solution.py:126
  (81 shorter events, 9.1 us)
Async XLA Ops:
  6.5 118.9 %copy-start = (bf16[768,1536]{1,0:T(8,128)(2,1)S(1)}, bf16[768,1536]{1,0:T(8,128)(2,1)}, u32[]{:S(2)}) copy-start(bf16[768,1536]{1,0:T(8,128)(2,1)} %param.17) | copy-start | bytes 7077892
  6.5 110.0 %all-gather.5.cloned.1.call-start = ((), (), s32[]{:S(2)}) async-start(), calls=%async_computation | async-start | bytes 3342336 | tf_op jit(solution)/shard_map/all_gather | solution.py:81
  10.4 5.0 %copy-start.3 = (bf16[1536,256]{1,0:T(8,128)(2,1)S(1)}, bf16[1536,256]{1,0:T(8,128)(2,1)}, u32[]{:S(2)}) copy-start(bf16[1536,256]{1,0:T(8,128)(2,1)} %param.15) | copy-start | bytes 2359300
  13.3 112.2 %all-gather.7.cloned.1.call-start = ((), (), s32[]{:S(2)}) async-start(), calls=%async_computation.1 | async-start | bytes 5013504 | tf_op jit(solution)/shard_map/all_gather | solution.py:53
  14.1 155.2 %all-gather.9.cloned.1.call-start = ((), (), s32[]{:S(2)}) async-start(), calls=%async_computation.2 | async-start | bytes 4177920 | tf_op jit(solution)/shard_map/all_gather | solution.py:54
  14.8 209.1 %all-gather.11.cloned.1.call-start = ((), (), s32[]{:S(2)}) async-start(), calls=%async_computation.3 | async-start | bytes 5013504 | tf_op jit(solution)/shard_map/all_gather | solution.py:55
  15.4 49.2 %copy-start.4 = (bf16[1536,256]{1,0:T(8,128)(2,1)S(1)}, bf16[1536,256]{1,0:T(8,128)(2,1)}, u32[]{:S(2)}) copy-start(bf16[1536,256]{1,0:T(8,128)(2,1)} %param.14) | copy-start | bytes 2359300
  15.7 0.6 copy-start.6
  15.7 7.6 %collective-permute-start = (bf16[2,64,256]{2,1,0:T(8,128)(2,1)S(1)}, bf16[2,64,256]{2,1,0:T(8,128)(2,1)S(1)}, u32[]{:S(2)}, u32[]{:S(2)}) collective-permute-start(bf16[2,64,256]{2,1,0:T(8,128)(2,1)S(1)} %bitcast.47), channel_id=1, source_target_pairs={{0,1},{1,2},{2,3},{3,4},{4,5},{5,6},{6,7},{7,8},{8,9},{9,10},{10,1... | collective-permute-start | bytes 196616 | tf_op jit(solution)/shard_map/ppermute | solution.py:20
  16.3 7.4 %collective-permute-start.1 = (bf16[2,64,256]{2,1,0:T(8,128)(2,1)S(1)}, bf16[2,64,256]{2,1,0:T(8,128)(2,1)S(1)}, u32[]{:S(2)}, u32[]{:S(2)}) collective-permute-start(bf16[2,64,256]{2,1,0:T(8,128)(2,1)S(1)} %bitcast.48), channel_id=1, source_target_pairs={{0,15},{1,0},{2,1},{3,2},{4,3},{5,4},{6,5},{7,6},{8,7},{9,8},{10,9... | collective-permute-start | bytes 196616 | tf_op jit(solution)/shard_map/ppermute | solution.py:25
  21.7 43.2 %copy-start.7 = (bf16[128,256]{1,0:T(8,128)(2,1)S(1)}, bf16[128,256]{1,0:T(8,128)(2,1)}, u32[]{:S(2)}) copy-start(bf16[128,256]{1,0:T(8,128)(2,1)} %copy-done.6) | copy-start | bytes 196612
  23.2 13.4 %copy-start.10 = (bf16[2,64,256]{2,1,0:T(8,128)(2,1)}, bf16[2,64,256]{2,1,0:T(8,128)(2,1)S(1)}, u32[]{:S(2)}) copy-start(bf16[2,64,256]{2,1,0:T(8,128)(2,1)S(1)} %collective-permute-done) | copy-start | bytes 196612
  23.2 6.6 %collective-permute-start.2 = (bf16[2,64,256]{2,1,0:T(8,128)(2,1)S(1)}, bf16[2,64,256]{2,1,0:T(8,128)(2,1)S(1)}, u32[]{:S(2)}, u32[]{:S(2)}) collective-permute-start(bf16[2,64,256]{2,1,0:T(8,128)(2,1)S(1)} %collective-permute-done), channel_id=1, source_target_pairs={{0,1},{1,2},{2,3},{3,4},{4,5},{5,6},{6,7},{7,8},{8,9},{9,10},{10,1... | collective-permute-start | bytes 196616 | tf_op jit(solution)/shard_map/ppermute | solution.py:20
  23.6 41.0 %copy-start.8 = (bf16[2,64,256]{2,1,0:T(8,128)(2,1)}, bf16[2,64,256]{2,1,0:T(8,128)(2,1)S(1)}, u32[]{:S(2)}) copy-start(bf16[2,64,256]{2,1,0:T(8,128)(2,1)S(1)} %collective-permute-done.1) | copy-start | bytes 196612
  23.6 7.4 %collective-permute-start.3 = (bf16[2,64,256]{2,1,0:T(8,128)(2,1)S(1)}, bf16[2,64,256]{2,1,0:T(8,128)(2,1)S(1)}, u32[]{:S(2)}, u32[]{:S(2)}) collective-permute-start(bf16[2,64,256]{2,1,0:T(8,128)(2,1)S(1)} %collective-permute-done.1), channel_id=1, source_target_pairs={{0,15},{1,0},{2,1},{3,2},{4,3},{5,4},{6,5},{7,6},{8,7},{9,8},{10,9... | collective-permute-start | bytes 196616 | tf_op jit(solution)/shard_map/ppermute | solution.py:25
  29.9 1.2 copy-start.9
  29.9 6.8 %collective-permute-start.4 = (bf16[2,64,256]{2,1,0:T(8,128)(2,1)S(1)}, bf16[2,64,256]{2,1,0:T(8,128)(2,1)S(1)}, u32[]{:S(2)}, u32[]{:S(2)}) collective-permute-start(bf16[2,64,256]{2,1,0:T(8,128)(2,1)S(1)} %collective-permute-done.2), channel_id=1, source_target_pairs={{0,1},{1,2},{2,3},{3,4},{4,5},{5,6},{6,7},{7,8},{8,9},{9,10},{10,1... | collective-permute-start | bytes 196616 | tf_op jit(solution)/shard_map/ppermute | solution.py:20
  31.0 5.6 %copy-start.11 = (bf16[2,64,256]{2,1,0:T(8,128)(2,1)}, bf16[2,64,256]{2,1,0:T(8,128)(2,1)S(1)}, u32[]{:S(2)}) copy-start(bf16[2,64,256]{2,1,0:T(8,128)(2,1)S(1)} %collective-permute-done.3) | copy-start | bytes 196612
  31.0 6.6 %collective-permute-start.5 = (bf16[2,64,256]{2,1,0:T(8,128)(2,1)S(1)}, bf16[2,64,256]{2,1,0:T(8,128)(2,1)S(1)}, u32[]{:S(2)}, u32[]{:S(2)}) collective-permute-start(bf16[2,64,256]{2,1,0:T(8,128)(2,1)S(1)} %collective-permute-done.3), channel_id=1, source_target_pairs={{0,15},{1,0},{2,1},{3,2},{4,3},{5,4},{6,5},{7,6},{8,7},{9,8},{10,9... | collective-permute-start | bytes 196616 | tf_op jit(solution)/shard_map/ppermute | solution.py:25
  36.7 1.0 copy-start.12
  36.7 6.5 %collective-permute-start.6 = (bf16[2,64,256]{2,1,0:T(8,128)(2,1)S(1)}, bf16[2,64,256]{2,1,0:T(8,128)(2,1)S(1)}, u32[]{:S(2)}, u32[]{:S(2)}) collective-permute-start(bf16[2,64,256]{2,1,0:T(8,128)(2,1)S(1)} %collective-permute-done.4), channel_id=1, source_target_pairs={{0,1},{1,2},{2,3},{3,4},{4,5},{5,6},{6,7},{7,8},{8,9},{9,10},{10,1... | collective-permute-start | bytes 196616 | tf_op jit(solution)/shard_map/ppermute | solution.py:20
  37.6 5.5 %copy-start.13 = (bf16[2,64,256]{2,1,0:T(8,128)(2,1)}, bf16[2,64,256]{2,1,0:T(8,128)(2,1)S(1)}, u32[]{:S(2)}) copy-start(bf16[2,64,256]{2,1,0:T(8,128)(2,1)S(1)} %collective-permute-done.5) | copy-start | bytes 196612
  37.6 7.4 %collective-permute-start.7 = (bf16[2,64,256]{2,1,0:T(8,128)(2,1)S(1)}, bf16[2,64,256]{2,1,0:T(8,128)(2,1)S(1)}, u32[]{:S(2)}, u32[]{:S(2)}) collective-permute-start(bf16[2,64,256]{2,1,0:T(8,128)(2,1)S(1)} %collective-permute-done.5), channel_id=1, source_target_pairs={{0,15},{1,0},{2,1},{3,2},{4,3},{5,4},{6,5},{7,6},{8,7},{9,8},{10,9... | collective-permute-start | bytes 196616 | tf_op jit(solution)/shard_map/ppermute | solution.py:25
  43.2 1.8 copy-start.14
  43.2 7.6 %collective-permute-start.8 = (bf16[2,64,256]{2,1,0:T(8,128)(2,1)S(1)}, bf16[2,64,256]{2,1,0:T(8,128)(2,1)S(1)}, u32[]{:S(2)}, u32[]{:S(2)}) collective-permute-start(bf16[2,64,256]{2,1,0:T(8,128)(2,1)S(1)} %collective-permute-done.6), channel_id=1, source_target_pairs={{0,1},{1,2},{2,3},{3,4},{4,5},{5,6},{6,7},{7,8},{8,9},{9,10},{10,1... | collective-permute-start | bytes 196616 | tf_op jit(solution)/shard_map/ppermute | solution.py:20
  45.0 5.8 %copy-start.15 = (bf16[2,64,256]{2,1,0:T(8,128)(2,1)}, bf16[2,64,256]{2,1,0:T(8,128)(2,1)S(1)}, u32[]{:S(2)}) copy-start(bf16[2,64,256]{2,1,0:T(8,128)(2,1)S(1)} %collective-permute-done.7) | copy-start | bytes 196612
  45.0 6.9 %collective-permute-start.9 = (bf16[2,64,256]{2,1,0:T(8,128)(2,1)S(1)}, bf16[2,64,256]{2,1,0:T(8,128)(2,1)S(1)}, u32[]{:S(2)}, u32[]{:S(2)}) collective-permute-start(bf16[2,64,256]{2,1,0:T(8,128)(2,1)S(1)} %collective-permute-done.7), channel_id=1, source_target_pairs={{0,15},{1,0},{2,1},{3,2},{4,3},{5,4},{6,5},{7,6},{8,7},{9,8},{10,9... | collective-permute-start | bytes 196616 | tf_op jit(solution)/shard_map/ppermute | solution.py:25
  50.8 1.1 copy-start.16
  50.8 6.7 %collective-permute-start.10 = (bf16[2,64,256]{2,1,0:T(8,128)(2,1)S(1)}, bf16[2,64,256]{2,1,0:T(8,128)(2,1)S(1)}, u32[]{:S(2)}, u32[]{:S(2)}) collective-permute-start(bf16[2,64,256]{2,1,0:T(8,128)(2,1)S(1)} %collective-permute-done.8), channel_id=1, source_target_pairs={{0,1},{1,2},{2,3},{3,4},{4,5},{5,6},{6,7},{7,8},{8,9},{9,10},{10,1... | collective-permute-start | bytes 196616 | tf_op jit(solution)/shard_map/ppermute | solution.py:20
  51.9 13.0 %copy-start.17 = (bf16[2,64,256]{2,1,0:T(8,128)(2,1)}, bf16[2,64,256]{2,1,0:T(8,128)(2,1)S(1)}, u32[]{:S(2)}) copy-start(bf16[2,64,256]{2,1,0:T(8,128)(2,1)S(1)} %collective-permute-done.9) | copy-start | bytes 196612
  51.9 8.1 %collective-permute-start.11 = (bf16[2,64,256]{2,1,0:T(8,128)(2,1)S(1)}, bf16[2,64,256]{2,1,0:T(8,128)(2,1)}, u32[]{:S(2)}, u32[]{:S(2)}) collective-permute-start(bf16[2,64,256]{2,1,0:T(8,128)(2,1)S(1)} %collective-permute-done.9), channel_id=1, source_target_pairs={{0,15},{1,0},{2,1},{3,2},{4,3},{5,4},{6,5},{7,6},{8,7},{9,8},{10,9... | collective-permute-start | bytes 196616 | tf_op jit(solution)/shard_map/ppermute | solution.py:25
  57.5 7.4 %copy-start.18 = (bf16[2,64,256]{2,1,0:T(8,128)(2,1)}, bf16[2,64,256]{2,1,0:T(8,128)(2,1)S(1)}, u32[]{:S(2)}) copy-start(bf16[2,64,256]{2,1,0:T(8,128)(2,1)S(1)} %collective-permute-done.10) | copy-start | bytes 196612
  57.5 7.1 %collective-permute-start.12 = (bf16[2,64,256]{2,1,0:T(8,128)(2,1)S(1)}, bf16[2,64,256]{2,1,0:T(8,128)(2,1)}, u32[]{:S(2)}, u32[]{:S(2)}) collective-permute-start(bf16[2,64,256]{2,1,0:T(8,128)(2,1)S(1)} %collective-permute-done.10), channel_id=1, source_target_pairs={{0,1},{1,2},{2,3},{3,4},{4,5},{5,6},{6,7},{7,8},{8,9},{9,10},{10,1... | collective-permute-start | bytes 196616 | tf_op jit(solution)/shard_map/ppermute | solution.py:20
  59.9 48.0 %collective-permute-start.13 = (bf16[2,64,256]{2,1,0:T(8,128)(2,1)}, bf16[2,64,256]{2,1,0:T(8,128)(2,1)}, u32[]{:S(2)}, u32[]{:S(2)}) collective-permute-start(bf16[2,64,256]{2,1,0:T(8,128)(2,1)} %collective-permute-done.11), channel_id=1, source_target_pairs={{0,15},{1,0},{2,1},{3,2},{4,3},{5,4},{6,5},{7,6},{8,7},{9,8},{10,9... | collective-permute-start | bytes 196616 | tf_op jit(solution)/shard_map/ppermute | solution.py:25
  64.6 46.7 %collective-permute-start.14 = (bf16[2,64,256]{2,1,0:T(8,128)(2,1)}, bf16[2,64,256]{2,1,0:T(8,128)(2,1)}, u32[]{:S(2)}, u32[]{:S(2)}) collective-permute-start(bf16[2,64,256]{2,1,0:T(8,128)(2,1)} %collective-permute-done.12), channel_id=1, source_target_pairs={{0,1},{1,2},{2,3},{3,4},{4,5},{5,6},{6,7},{7,8},{8,9},{9,10},{10,1... | collective-permute-start | bytes 196616 | tf_op jit(solution)/shard_map/ppermute | solution.py:20
  114.6 1.4 copy-start.1
  121.3 4.2 %copy-start.2 = (bf16[2,64,1536]{2,1,0:T(8,128)(2,1)S(1)}, bf16[2,64,1536]{2,1,0:T(8,128)(2,1)}, u32[]{:S(2)}) copy-start(bf16[2,64,1536]{2,1,0:T(8,128)(2,1)} %param.11) | copy-start | bytes 1179652
  130.8 38.5 %copy-start.5 = (bf16[2,128,1280]{2,1,0:T(8,128)(2,1)S(1)}, bf16[2,128,1280]{2,1,0:T(8,128)(2,1)}, u32[]{:S(2)}) copy-start(bf16[2,128,1280]{2,1,0:T(8,128)(2,1)} %fusion.13) | copy-start | bytes 1966084
  169.3 7.3 %copy-start.19 = (f32[3,1536]{1,0:T(4,128)S(1)}, f32[3,1536]{1,0:T(4,128)}, u32[]{:S(2)}) copy-start(f32[3,1536]{1,0:T(4,128)} %param.20) | copy-start | bytes 55300
  173.1 3.5 %collective-permute-start.15 = (bf16[2,1,1536]{2,1,0:T(2,128)(2,1)S(1)}, bf16[2,1,1536]{2,1,0:T(2,128)(2,1)S(1)}, u32[]{:S(2)}, u32[]{:S(2)}) collective-permute-start(bf16[2,1,1536]{2,1,0:T(2,128)(2,1)S(1)} %get-tuple-element.8), channel_id=1, source_target_pairs={{0,1},{1,2},{2,3},{3,4},{4,5},{5,6},{6,7},{7,8},{8,9},{9,10},{10,1... | collective-permute-start | bytes 18440 | tf_op jit(solution)/shard_map/ppermute | solution.py:40
  175.2 3.1 %collective-permute-start.16 = (bf16[2,1,1536]{2,1,0:T(2,128)(2,1)S(1)}, bf16[2,1,1536]{2,1,0:T(2,128)(2,1)S(1)}, u32[]{:S(2)}, u32[]{:S(2)}) collective-permute-start(bf16[2,1,1536]{2,1,0:T(2,128)(2,1)S(1)} %get-tuple-element.9), channel_id=1, source_target_pairs={{1,0},{2,1},{3,2},{4,3},{5,4},{6,5},{7,6},{8,7},{9,8},{10,9},{11,1... | collective-permute-start | bytes 18440 | tf_op jit(solution)/shard_map/ppermute | solution.py:42
Sparse Core Ops, SparseCore 0:
  13.4 50.8 all-gather.4
  66.6 52.9 all-gather.6
  121.9 47.3 all-gather.8
  171.4 52.4 all-gather.10
